TPU v7x, 32 devices: a whole 2x2x4 slice. The times are simulated.
32 devices in a mesh: groups: 2 (over x), outer: 4 (over z), inner: 4 (over y, core).
Axes of the slice: x: 2, y: 2, z: 4, core: 2. Of those that a mesh axis runs over, the one named last changes fastest.
Arguments:
- q_proj: bfloat16 [16384, 2048], P(('groups', 'outer', 'inner')), parts along dimension 0, may hold values from -4 to 4
- k_proj: bfloat16 [16384, 512], P(('groups', 'outer', 'inner')), parts along dimension 0, may hold values from -4 to 4
- v_proj: bfloat16 [16384, 512], P(('groups', 'outer', 'inner')), parts along dimension 0, may hold values from -6 to 6
- q_taps: float32 [3, 2048], replicated, may hold values from 0.5 to 1.5
- k_taps: float32 [3, 512], replicated, may hold values from 0.5 to 1.5
- v_taps: float32 [3, 512], replicated, may hold values from 0.5 to 1.5
- block_list: int32 [128, 3], P(('groups', 'outer', 'inner')), parts along dimension 0, may hold values from -1 to 63, as said below
Outputs:
- attn_out: bfloat16 [16384, 2048], P(('groups', 'outer', 'inner')), parts along dimension 0
There are 2 independent parts, one for each index of `groups`. A program takes and returns all parts, laid end to end along the dimension named above; an argument that names none is the same for every part. Nothing has to cross between parts.
Inputs may be any that keep to these rules, and one draw needn't show every extreme that they name: `block_list`: row a holds block a and the 1 block before it that exist, then every block b <= a - 2 with b % 64 equal to a phase shared by all rows of a part, the phase below 62; all other entries are -1, and the last row has none.
All inputs are finite; a program needn't handle non-finite values.
Results may differ from a plain program's by a relative error of at most 0.002.
The roundings to bfloat16 on the way count: a program that leaves them out, or rounds other values in their place, can miss the bound.
Values may be sent and summed in bfloat16 or wider, within the bound.
A program may use at most 64 MiB of HBM per device.

v0:
```python
import math

import jax
import jax.numpy as jnp
from jax import lax
from jax.sharding import PartitionSpec as P

HEAD_DIM = 128
BLOCK = 128
LOCAL = 2
STRIDE = 64
KERNEL = 3


def shifted(block, axis, distance):
    devices = range(lax.axis_size(axis))
    route = [(i - distance, i) for i in devices if i - distance in devices]
    return lax.ppermute(block, axis, route)


def causal_conv(source, kernel_taps, before):
    width = kernel_taps.shape[0]
    row_count = source.shape[0]
    joined = jnp.concatenate([before, source], 0)
    summed = jnp.zeros((row_count, source.shape[1]), jnp.float32)
    for offset in range(width):
        start = width - 1 - offset
        summed = summed + kernel_taps[offset][None, :] * joined[start : start + row_count].astype(
            jnp.float32
        )
    return summed.astype(jnp.bfloat16)


def body(q_proj, k_proj, v_proj, q_taps, k_taps, v_taps, block_list):
    tokens_here = q_proj.shape[0]
    per_dev = tokens_here // BLOCK
    kv_width = k_proj.shape[1]
    inner_count = lax.axis_size("inner")
    outer_count = lax.axis_size("outer")
    device = lax.axis_index("outer") * inner_count + lax.axis_index("inner")
    rim_rows = KERNEL - 1
    window_rows = (LOCAL - 1) * BLOCK
    query_rim, key_rim, value_rim = shifted(
        (
            q_proj[tokens_here - rim_rows :],
            k_proj[tokens_here - rim_rows :],
            v_proj[tokens_here - rim_rows :],
        ),
        ("outer", "inner"),
        1,
    )
    q_conv = causal_conv(q_proj, q_taps, query_rim)
    k_conv = causal_conv(k_proj, k_taps, key_rim)
    v_conv = causal_conv(v_proj, v_taps, value_rim)
    prev_keys, prev_values = shifted(
        (k_conv[tokens_here - window_rows :], v_conv[tokens_here - window_rows :]),
        ("outer", "inner"),
        1,
    )
    first_block = device * per_dev
    query_ids = first_block + jnp.arange(per_dev, dtype=jnp.int32)
    distant = (block_list >= 0) & (block_list <= query_ids[:, None] - LOCAL)
    phase_guess = jnp.max(jnp.where(distant, block_list % STRIDE, -1))
    phase_id = lax.pmax(phase_guess, ("outer", "inner"))
    period = STRIDE // per_dev
    base_col = phase_id // per_dev % period % inner_count
    local_pos = phase_id % per_dev
    per_row = max(1, inner_count // period)
    owner_cols = base_col + period * jnp.arange(per_row, dtype=jnp.int32)
    cand_keys = lax.dynamic_slice_in_dim(k_conv, local_pos * BLOCK, BLOCK, 0)
    cand_values = lax.dynamic_slice_in_dim(v_conv, local_pos * BLOCK, BLOCK, 0)
    row_keys, row_values = (
        lax.all_gather(cand_keys, "inner", axis=0, tiled=True),
        lax.all_gather(cand_values, "inner", axis=0, tiled=True),
    )
    pick_keys = jnp.take(row_keys.reshape(inner_count, BLOCK, kv_width), owner_cols, axis=0)
    pick_values = jnp.take(row_values.reshape(inner_count, BLOCK, kv_width), owner_cols, axis=0)
    far_keys, far_values = (
        lax.all_gather(pick_keys, "outer", axis=0, tiled=True),
        lax.all_gather(pick_values, "outer", axis=0, tiled=True),
    )
    owners = (
        jnp.arange(outer_count, dtype=jnp.int32)[:, None] * inner_count + owner_cols[None, :]
    ).reshape(-1)
    far_keys = far_keys.reshape(-1, kv_width)
    far_values = far_values.reshape(-1, kv_width)
    far_ids = owners * per_dev + local_pos
    all_keys = jnp.concatenate([prev_keys, k_conv, far_keys], 0)
    all_values = jnp.concatenate([prev_values, v_conv, far_values], 0)
    near_ids = first_block - (LOCAL - 1) + jnp.arange(LOCAL - 1, dtype=jnp.int32)
    all_ids = jnp.concatenate([near_ids, query_ids, far_ids], 0)
    block_total = all_ids.shape[0]
    listed = jnp.any(
        (block_list[:, None, :] == all_ids[None, :, None]) & (block_list >= 0)[:, None, :], axis=2
    )
    beyond = jnp.concatenate(
        [jnp.ones((LOCAL - 1 + per_dev,), bool), far_ids < first_block - (LOCAL - 1)], 0
    )
    allowed = listed & beyond[None, :]
    key_pos = (all_ids[:, None] * BLOCK + jnp.arange(BLOCK, dtype=jnp.int32)[None, :]).reshape(-1)
    query_pos = device * tokens_here + jnp.arange(tokens_here, dtype=jnp.int32)
    visible = jnp.broadcast_to(allowed[:, None, :, None], (per_dev, BLOCK, block_total, BLOCK))
    visible = visible.reshape(tokens_here, block_total * BLOCK) & (
        key_pos[None, :] <= query_pos[:, None]
    )
    head_count = q_proj.shape[1] // HEAD_DIM
    per_group = head_count // (kv_width // HEAD_DIM)
    inv_scale = 1.0 / math.sqrt(HEAD_DIM)

    def head_step(head, output):
        query_cols = lax.dynamic_slice_in_dim(q_conv, head * HEAD_DIM, HEAD_DIM, 1)
        group_id = head // per_group
        key_cols = lax.dynamic_slice_in_dim(all_keys, group_id * HEAD_DIM, HEAD_DIM, 1)
        value_cols = lax.dynamic_slice_in_dim(all_values, group_id * HEAD_DIM, HEAD_DIM, 1)
        scores = (
            lax.dot_general(
                query_cols, key_cols, (((1,), (1,)), ((), ())), preferred_element_type=jnp.float32
            )
            * inv_scale
        )
        scores = jnp.where(visible, scores, -1e30)
        peak = jnp.max(scores, axis=1, keepdims=True)
        terms = jnp.where(visible, jnp.exp(scores - peak), 0.0)
        totals = jnp.sum(terms, axis=1, keepdims=True)
        rounded = terms.astype(jnp.bfloat16)
        mixed = jnp.dot(rounded, value_cols, preferred_element_type=jnp.float32)
        return lax.dynamic_update_slice_in_dim(
            output, (mixed / totals).astype(jnp.bfloat16), head * HEAD_DIM, 1
        )

    attn_out = jnp.zeros((tokens_here, q_proj.shape[1]), jnp.bfloat16)
    return lax.fori_loop(0, head_count, head_step, attn_out)


def solution(mesh):
    return jax.shard_map(
        body,
        mesh=mesh,
        in_specs=(
            P(("groups", "outer", "inner"), None),
            P(("groups", "outer", "inner"), None),
            P(("groups", "outer", "inner"), None),
            P(),
            P(),
            P(),
            P(("groups", "outer", "inner"), None),
        ),
        out_specs=P(("groups", "outer", "inner"), None),
        check_vma=False,
    )
```

profile of v0, /device:TPU:0, one launch (start us, length us, event | category | flops | bytes accessed | tf_op | source)
XLA Modules:
  0.0 177.0 jit_solution(12822102147347245752)
XLA Ops:
  0.7 2.3 %collective-permute-start.3 = (bf16[2,512]{1,0:T(2,128)(2,1)S(1)}, bf16[2,512]{1,0:T(2,128)(2,1)S(1)}, u32[]{:S(2)}, u32[]{:S(2)}) collective-permute-start(bf16[2,512]{1,0:T(2,128)(2,1)S(1)} %slice.75), channel_id=1, source_target_pairs={{0,1},{1,2},{2,3},{3,4},{4,5},{5,6},{6,7},{7,8},{8,9},{9,10},{10,1... | collective-permute-start | bytes 6152 | tf_op jit(solution)/shard_map/ppermute | solution.py:18
  3.8 4.5 %collective-permute-start.1 = (bf16[2,512]{1,0:T(2,128)(2,1)S(1)}, bf16[2,512]{1,0:T(2,128)(2,1)S(1)}, u32[]{:S(2)}, u32[]{:S(2)}) collective-permute-start(bf16[2,512]{1,0:T(2,128)(2,1)S(1)} %slice.68), channel_id=1, source_target_pairs={{0,1},{1,2},{2,3},{3,4},{4,5},{5,6},{6,7},{7,8},{8,9},{9,10},{10,1... | collective-permute-start | bytes 6152 | tf_op jit(solution)/shard_map/ppermute | solution.py:18
  9.1 1.9 %collective-permute-start = (bf16[2,2048]{1,0:T(2,128)(2,1)S(1)}, bf16[2,2048]{1,0:T(2,128)(2,1)S(1)}, u32[]{:S(2)}, u32[]{:S(2)}) collective-permute-start(bf16[2,2048]{1,0:T(2,128)(2,1)S(1)} %slice.62), channel_id=1, source_target_pairs={{0,1},{1,2},{2,3},{3,4},{4,5},{5,6},{6,7},{7,8},{8,9},{9,10},{10,1... | collective-permute-start | bytes 24584 | tf_op jit(solution)/shard_map/ppermute | solution.py:18
  13.1 12.3 %pmax.7 = s32[]{:T(128)} all-reduce(s32[]{:T(128)} %fusion.29), channel_id=1, replica_groups=mesh['groups'=2,'outer'=4,'inner'=4] {'outer','inner'}, use_global_device_ids=true, to_apply=%region_1.2 | all-reduce | flops 1 | bytes 8 | tf_op jit(solution)/shard_map/pmax | solution.py:64
  31.9 2.1 %add_convert_fusion.2 = bf16[512,512]{1,0:T(8,128)(2,1)S(1)} fusion(bf16[512,512]{1,0:T(8,128)(2,1)} %param.12, bf16[2,512]{1,0:T(2,128)(2,1)S(1)} %collective-permute-done.1, f32[512]{0:T(512)S(1)} %bitcast.45, f32[512]{0:T(512)S(1)} %bitcast.46, f32[512]{0:T(512)S(1)} %bitcast.44), kind=kLoop, calls=%fused_computation.28 | loop fusion | flops 3932160 | bytes 1056768 | tf_op jit(solution)/shard_map/convert_element_type | solution.py:31
  35.3 1.9 %add_convert_fusion.1 = bf16[512,512]{1,0:T(8,128)(2,1)S(1)} fusion(bf16[512,512]{1,0:T(8,128)(2,1)} %param.13, bf16[2,512]{1,0:T(2,128)(2,1)S(1)} %collective-permute-done.3, f32[512]{0:T(512)S(1)} %bitcast.42, f32[512]{0:T(512)S(1)} %bitcast.43, f32[512]{0:T(512)S(1)} %bitcast.41), kind=kLoop, calls=%fused_computation.27 | loop fusion | flops 3932160 | bytes 1056768 | tf_op jit(solution)/shard_map/convert_element_type | solution.py:31
  37.3 3.8 %collective-permute-start.4 = (bf16[128,512]{1,0:T(8,128)(2,1)S(1)}, bf16[128,512]{1,0:T(8,128)(2,1)S(1)}, u32[]{:S(2)}, u32[]{:S(2)}) collective-permute-start(bf16[128,512]{1,0:T(8,128)(2,1)S(1)} %get-tuple-element.224), channel_id=1, source_target_pairs={{0,1},{1,2},{2,3},{3,4},{4,5},{5,6},{6,7},{7,8},{8,9},{9,10},{10,1... | collective-permute-start | bytes 393224 | tf_op jit(solution)/shard_map/ppermute | solution.py:18
  41.1 8.2 %all_gather.14 = bf16[512,512]{1,0:T(8,128)(2,1)S(1)} all-gather(bf16[128,512]{1,0:T(8,128)(2,1)S(1)} %get-tuple-element.225), channel_id=1, replica_groups=mesh['groups'=2,'outer'=4,'inner'=4] {'inner'}, dimensions={0}, use_global_device_ids=true | all-gather | bytes 655360 | tf_op jit(solution)/shard_map/all_gather | solution.py:74
  49.4 16.1 %all_gather.15 = bf16[4,128,512]{2,1,0:T(8,128)(2,1)S(1)} all-gather(bf16[1,128,512]{2,1,0:T(8,128)(2,1)S(1)} %dynamic-slice_select_fusion), channel_id=1, replica_groups=mesh['groups'=2,'outer'=4,'inner'=4] {'outer'}, dimensions={0}, use_global_device_ids=true | all-gather | bytes 655360 | tf_op jit(solution)/shard_map/all_gather | solution.py:80
  65.6 7.0 %all_gather.12 = bf16[512,512]{1,0:T(8,128)(2,1)S(1)} all-gather(bf16[128,512]{1,0:T(8,128)(2,1)S(1)} %get-tuple-element.227), channel_id=1, replica_groups=mesh['groups'=2,'outer'=4,'inner'=4] {'inner'}, dimensions={0}, use_global_device_ids=true | all-gather | bytes 655360 | tf_op jit(solution)/shard_map/all_gather | solution.py:73
  72.6 16.2 %all_gather.13 = bf16[4,128,512]{2,1,0:T(8,128)(2,1)S(1)} all-gather(bf16[1,128,512]{2,1,0:T(8,128)(2,1)S(1)} %dynamic-slice_select_fusion.1), channel_id=1, replica_groups=mesh['groups'=2,'outer'=4,'inner'=4] {'outer'}, dimensions={0}, use_global_device_ids=true | all-gather | bytes 655360 | tf_op jit(solution)/shard_map/all_gather | solution.py:79
  88.8 2.6 %add_convert_fusion = bf16[512,2048]{1,0:T(8,128)(2,1)} fusion(bf16[512,2048]{1,0:T(8,128)(2,1)S(1)} %copy-done, bf16[2,2048]{1,0:T(2,128)(2,1)S(1)} %collective-permute-done, f32[2048]{0:T(1024)S(1)} %bitcast.39, f32[2048]{0:T(1024)S(1)} %bitcast.40, f32[2048]{0:T(1024)S(1)} %bitcast.38), kind=kLoop, calls=%fused_computation.20 | loop fusion | flops 15728640 | bytes 4227072 | tf_op jit(solution)/shard_map/convert_element_type | solution.py:31
  92.9 82.8 %while.17 = (s32[]{:T(128)}, bf16[512,2048]{1,0:T(8,128)(2,1)S(1)}, bf16[512,2048]{1,0:T(8,128)(2,1)}, bf16[1152,512]{1,0:T(8,128)(2,1)}, bf16[1152,512]{1,0:T(8...) while((s32[]{:T(128)}, bf16[512,2048]{1,0:T(8,128)(2,1)S(1)}, ...), condition=%wide.region_6.8_spmd.clone, body=%wide.region_3.7_spmd.clone.sunk | while | flops 310967296 | bytes 12682619 | solution.py:132
  94.3 1.9 %fusion.43 = (f32[512]{0:T(512)S(1)}, f32[512,1152]{1,0:T(8,128)S(1)}) fusion(bf16[1152,512]{1,0:T(8,128)(2,1)} %get-tuple-element.325, s32[]{:T(128)S(6)} %select_n.153, bf16[512,2048]{1,0:T(8,128)(2,1)} %get-tuple-element.324, s32[]{:T(128)S(6)} %select_n.151, pred[512,1152]{1,0:T(32,128)(4,1)S(1)} %copy.20, s32[512]{0:T(512)S(1)} %get-tuple-element.328, ...), kind=kOutput, calls=%fused_computation.58.clone.1 | convolution fusion | flops 153943552 | bytes 3383816 | tf_op jit(solution)/shard_map/while/body/eval_jaxpr/dot_general | solution.py:116
  99.5 1.9 %fusion.43 = (f32[512]{0:T(512)S(1)}, f32[512,1152]{1,0:T(8,128)S(1)}) fusion(bf16[1152,512]{1,0:T(8,128)(2,1)} %get-tuple-element.325, s32[]{:T(128)S(6)} %select_n.153, bf16[512,2048]{1,0:T(8,128)(2,1)} %get-tuple-element.324, s32[]{:T(128)S(6)} %select_n.151, pred[512,1152]{1,0:T(32,128)(4,1)S(1)} %copy.20, s32[512]{0:T(512)S(1)} %get-tuple-element.328, ...), kind=kOutput, calls=%fused_computation.58.clone.1 | convolution fusion | flops 153943552 | bytes 3383816 | tf_op jit(solution)/shard_map/while/body/eval_jaxpr/dot_general | solution.py:116
  104.7 1.9 %fusion.43 = (f32[512]{0:T(512)S(1)}, f32[512,1152]{1,0:T(8,128)S(1)}) fusion(bf16[1152,512]{1,0:T(8,128)(2,1)} %get-tuple-element.325, s32[]{:T(128)S(6)} %select_n.153, bf16[512,2048]{1,0:T(8,128)(2,1)} %get-tuple-element.324, s32[]{:T(128)S(6)} %select_n.151, pred[512,1152]{1,0:T(32,128)(4,1)S(1)} %copy.20, s32[512]{0:T(512)S(1)} %get-tuple-element.328, ...), kind=kOutput, calls=%fused_computation.58.clone.1 | convolution fusion | flops 153943552 | bytes 3383816 | tf_op jit(solution)/shard_map/while/body/eval_jaxpr/dot_general | solution.py:116
  109.8 1.9 %fusion.43 = (f32[512]{0:T(512)S(1)}, f32[512,1152]{1,0:T(8,128)S(1)}) fusion(bf16[1152,512]{1,0:T(8,128)(2,1)} %get-tuple-element.325, s32[]{:T(128)S(6)} %select_n.153, bf16[512,2048]{1,0:T(8,128)(2,1)} %get-tuple-element.324, s32[]{:T(128)S(6)} %select_n.151, pred[512,1152]{1,0:T(32,128)(4,1)S(1)} %copy.20, s32[512]{0:T(512)S(1)} %get-tuple-element.328, ...), kind=kOutput, calls=%fused_computation.58.clone.1 | convolution fusion | flops 153943552 | bytes 3383816 | tf_op jit(solution)/shard_map/while/body/eval_jaxpr/dot_general | solution.py:116
  115.0 1.9 %fusion.43 = (f32[512]{0:T(512)S(1)}, f32[512,1152]{1,0:T(8,128)S(1)}) fusion(bf16[1152,512]{1,0:T(8,128)(2,1)} %get-tuple-element.325, s32[]{:T(128)S(6)} %select_n.153, bf16[512,2048]{1,0:T(8,128)(2,1)} %get-tuple-element.324, s32[]{:T(128)S(6)} %select_n.151, pred[512,1152]{1,0:T(32,128)(4,1)S(1)} %copy.20, s32[512]{0:T(512)S(1)} %get-tuple-element.328, ...), kind=kOutput, calls=%fused_computation.58.clone.1 | convolution fusion | flops 153943552 | bytes 3383816 | tf_op jit(solution)/shard_map/while/body/eval_jaxpr/dot_general | solution.py:116
  130.5 1.9 %fusion.43 = (f32[512]{0:T(512)S(1)}, f32[512,1152]{1,0:T(8,128)S(1)}) fusion(bf16[1152,512]{1,0:T(8,128)(2,1)} %get-tuple-element.325, s32[]{:T(128)S(6)} %select_n.153, bf16[512,2048]{1,0:T(8,128)(2,1)} %get-tuple-element.324, s32[]{:T(128)S(6)} %select_n.151, pred[512,1152]{1,0:T(32,128)(4,1)S(1)} %copy.20, s32[512]{0:T(512)S(1)} %get-tuple-element.328, ...), kind=kOutput, calls=%fused_computation.58.clone.1 | convolution fusion | flops 153943552 | bytes 3383816 | tf_op jit(solution)/shard_map/while/body/eval_jaxpr/dot_general | solution.py:116
  140.9 1.9 %fusion.43 = (f32[512]{0:T(512)S(1)}, f32[512,1152]{1,0:T(8,128)S(1)}) fusion(bf16[1152,512]{1,0:T(8,128)(2,1)} %get-tuple-element.325, s32[]{:T(128)S(6)} %select_n.153, bf16[512,2048]{1,0:T(8,128)(2,1)} %get-tuple-element.324, s32[]{:T(128)S(6)} %select_n.151, pred[512,1152]{1,0:T(32,128)(4,1)S(1)} %copy.20, s32[512]{0:T(512)S(1)} %get-tuple-element.328, ...), kind=kOutput, calls=%fused_computation.58.clone.1 | convolution fusion | flops 153943552 | bytes 3383816 | tf_op jit(solution)/shard_map/while/body/eval_jaxpr/dot_general | solution.py:116
  146.1 1.9 %fusion.43 = (f32[512]{0:T(512)S(1)}, f32[512,1152]{1,0:T(8,128)S(1)}) fusion(bf16[1152,512]{1,0:T(8,128)(2,1)} %get-tuple-element.325, s32[]{:T(128)S(6)} %select_n.153, bf16[512,2048]{1,0:T(8,128)(2,1)} %get-tuple-element.324, s32[]{:T(128)S(6)} %select_n.151, pred[512,1152]{1,0:T(32,128)(4,1)S(1)} %copy.20, s32[512]{0:T(512)S(1)} %get-tuple-element.328, ...), kind=kOutput, calls=%fused_computation.58.clone.1 | convolution fusion | flops 153943552 | bytes 3383816 | tf_op jit(solution)/shard_map/while/body/eval_jaxpr/dot_general | solution.py:116
  156.4 1.9 %fusion.43 = (f32[512]{0:T(512)S(1)}, f32[512,1152]{1,0:T(8,128)S(1)}) fusion(bf16[1152,512]{1,0:T(8,128)(2,1)} %get-tuple-element.325, s32[]{:T(128)S(6)} %select_n.153, bf16[512,2048]{1,0:T(8,128)(2,1)} %get-tuple-element.324, s32[]{:T(128)S(6)} %select_n.151, pred[512,1152]{1,0:T(32,128)(4,1)S(1)} %copy.20, s32[512]{0:T(512)S(1)} %get-tuple-element.328, ...), kind=kOutput, calls=%fused_computation.58.clone.1 | convolution fusion | flops 153943552 | bytes 3383816 | tf_op jit(solution)/shard_map/while/body/eval_jaxpr/dot_general | solution.py:116
  166.7 1.9 %fusion.43 = (f32[512]{0:T(512)S(1)}, f32[512,1152]{1,0:T(8,128)S(1)}) fusion(bf16[1152,512]{1,0:T(8,128)(2,1)} %get-tuple-element.325, s32[]{:T(128)S(6)} %select_n.153, bf16[512,2048]{1,0:T(8,128)(2,1)} %get-tuple-element.324, s32[]{:T(128)S(6)} %select_n.151, pred[512,1152]{1,0:T(32,128)(4,1)S(1)} %copy.20, s32[512]{0:T(512)S(1)} %get-tuple-element.328, ...), kind=kOutput, calls=%fused_computation.58.clone.1 | convolution fusion | flops 153943552 | bytes 3383816 | tf_op jit(solution)/shard_map/while/body/eval_jaxpr/dot_general | solution.py:116
  171.9 1.9 %fusion.43 = (f32[512]{0:T(512)S(1)}, f32[512,1152]{1,0:T(8,128)S(1)}) fusion(bf16[1152,512]{1,0:T(8,128)(2,1)} %get-tuple-element.325, s32[]{:T(128)S(6)} %select_n.153, bf16[512,2048]{1,0:T(8,128)(2,1)} %get-tuple-element.324, s32[]{:T(128)S(6)} %select_n.151, pred[512,1152]{1,0:T(32,128)(4,1)S(1)} %copy.20, s32[512]{0:T(512)S(1)} %get-tuple-element.328, ...), kind=kOutput, calls=%fused_computation.58.clone.1 | convolution fusion | flops 153943552 | bytes 3383816 | tf_op jit(solution)/shard_map/while/body/eval_jaxpr/dot_general | solution.py:116
  (122 shorter events, 73.0 us)
Async XLA Ops:
  0.7 34.6 %collective-permute-start.3 = (bf16[2,512]{1,0:T(2,128)(2,1)S(1)}, bf16[2,512]{1,0:T(2,128)(2,1)S(1)}, u32[]{:S(2)}, u32[]{:S(2)}) collective-permute-start(bf16[2,512]{1,0:T(2,128)(2,1)S(1)} %slice.75), channel_id=1, source_target_pairs={{0,1},{1,2},{2,3},{3,4},{4,5},{5,6},{6,7},{7,8},{8,9},{9,10},{10,1... | collective-permute-start | bytes 6152 | tf_op jit(solution)/shard_map/ppermute | solution.py:18
  3.8 28.1 %collective-permute-start.1 = (bf16[2,512]{1,0:T(2,128)(2,1)S(1)}, bf16[2,512]{1,0:T(2,128)(2,1)S(1)}, u32[]{:S(2)}, u32[]{:S(2)}) collective-permute-start(bf16[2,512]{1,0:T(2,128)(2,1)S(1)} %slice.68), channel_id=1, source_target_pairs={{0,1},{1,2},{2,3},{3,4},{4,5},{5,6},{6,7},{7,8},{8,9},{9,10},{10,1... | collective-permute-start | bytes 6152 | tf_op jit(solution)/shard_map/ppermute | solution.py:18
  9.1 79.8 %collective-permute-start = (bf16[2,2048]{1,0:T(2,128)(2,1)S(1)}, bf16[2,2048]{1,0:T(2,128)(2,1)S(1)}, u32[]{:S(2)}, u32[]{:S(2)}) collective-permute-start(bf16[2,2048]{1,0:T(2,128)(2,1)S(1)} %slice.62), channel_id=1, source_target_pairs={{0,1},{1,2},{2,3},{3,4},{4,5},{5,6},{6,7},{7,8},{8,9},{9,10},{10,1... | collective-permute-start | bytes 24584 | tf_op jit(solution)/shard_map/ppermute | solution.py:18
  34.0 57.5 %collective-permute-start.2 = (bf16[128,512]{1,0:T(8,128)(2,1)S(1)}, bf16[128,512]{1,0:T(8,128)(2,1)S(1)}, u32[]{:S(2)}, u32[]{:S(2)}) collective-permute-start(bf16[128,512]{1,0:T(8,128)(2,1)S(1)} %get-tuple-element.226), channel_id=1, source_target_pairs={{0,1},{1,2},{2,3},{3,4},{4,5},{5,6},{6,7},{7,8},{8,9},{9,10},{10,1... | collective-permute-start | bytes 393224 | tf_op jit(solution)/shard_map/ppermute | solution.py:18
  35.3 53.5 %copy-start = (bf16[512,2048]{1,0:T(8,128)(2,1)S(1)}, bf16[512,2048]{1,0:T(8,128)(2,1)}, u32[]{:S(2)}) copy-start(bf16[512,2048]{1,0:T(8,128)(2,1)} %param.11) | copy-start | bytes 6291460
  37.3 54.1 %collective-permute-start.4 = (bf16[128,512]{1,0:T(8,128)(2,1)S(1)}, bf16[128,512]{1,0:T(8,128)(2,1)S(1)}, u32[]{:S(2)}, u32[]{:S(2)}) collective-permute-start(bf16[128,512]{1,0:T(8,128)(2,1)S(1)} %get-tuple-element.224), channel_id=1, source_target_pairs={{0,1},{1,2},{2,3},{3,4},{4,5},{5,6},{6,7},{7,8},{8,9},{9,10},{10,1... | collective-permute-start | bytes 393224 | tf_op jit(solution)/shard_map/ppermute | solution.py:18
  175.6 1.3 copy-start.1
where the time goes:
time: 178 us; the launch traced here: 177 us
  blocking collectives  59.9 us (34%)
  matrix products  44.9 us (25%)
  local copies, waits for them, and re-layouts  29.2 us (16%)
  other arithmetic  25.2 us (14%)
  starting transfers between devices  13.9 us (8%)
  between operations  2.83 us (2%)
    dot_general x16, matrix products, head_step(): lax.dot_general(query_cols, key_cols, (((1,), (1,)), ((), ())), preferred...  30.4 us
    all_gather x1, blocking collectives, body(): lax.all_gather(pick_keys, 'outer', axis=0, tiled=True)  16.2 us
    all_gather x1, blocking collectives, body(): lax.all_gather(pick_values, 'outer', axis=0, tiled=True)  16.1 us
    reduce_sum x16, other arithmetic, head_step(): totals = jnp.sum(terms, axis=1, keepdims=True)  15 us
    dot_general x16, matrix products, head_step(): mixed = jnp.dot(rounded, value_cols, preferred_element_type=jnp.float32)  14.4 us
    ppermute x5, starting transfers between devices, shifted(): return lax.ppermute(block, axis, route)  13.9 us
    pmax x1, blocking collectives, body(): phase_id = lax.pmax(phase_guess, ('outer', 'inner'))  12.3 us
    reshape x16, local copies, waits for them, and re-layouts, body(): visible.reshape(tokens_here, block_total * BLOCK)  11.3 us
  transfers between devices with their start and end apart: 5, of which 0 were waited for; matrix products, arithmetic and copies ran while one was open for 8% of the time, Pallas kernels for 0%

commit v1 on v0

v1 whole, which is shorter than its diff:
```python
import functools
import math

import jax
import jax.numpy as jnp
from jax import lax
from jax.experimental import pallas as pl
from jax.experimental.pallas import tpu as pltpu
from jax.sharding import PartitionSpec as P

HEAD_DIM = 128
BLOCK = 128
LOCAL = 2
STRIDE = 64
HALO = 16
NEG = -1e30
MESH = pl.DeviceIdType.MESH
SCALE = math.log2(math.e) / math.sqrt(HEAD_DIM)
NT = (((1,), (1,)), ((), ()))


def conv(padded, taps):
    wide = padded.astype(jnp.float32)
    total = taps[0:1] * wide[HALO:]
    for j in (1, 2):
        total = total + taps[j : j + 1] * pltpu.roll(wide, j, 0)[HALO:]
    return total.astype(jnp.bfloat16)


def kernel(
    ni, no, list_ref, q_hbm, k_hbm, v_hbm, qt_ref, kt_ref, vt_ref, out_hbm,
    qpad, kvpad, kvc, qs, acc_ref, max_ref, outb, wout, win, cand, rbuf, zpiece, zbuf,
    fsum, far, in_sem, tail_s, tail_r, win_s, win_r, w_s, w_r, sc_s, sc_r, z_s, z_r,
    g_s, g_r, out_sem,
):
    tokens, qw = q_hbm.shape
    kvw = k_hbm.shape[1]
    groups = kvw // HEAD_DIM
    per_group = qw // kvw
    nb = tokens // BLOCK
    slots = far.shape[0]
    piece = 2 * BLOCK // ni
    entries = list_ref.shape[1]
    o = lax.axis_index("outer")
    i = lax.axis_index("inner")
    d = o * ni + i
    last = ni * no - 1
    has_next = d < last
    has_prev = d > 0

    def chain(step):
        other = d + step
        return {"outer": other // ni, "inner": lax.rem(other, ni)}

    def inner_peer(r):
        return {"inner": lax.rem(i + r, ni)}

    loads = [
        pltpu.make_async_copy(q_hbm, qpad.at[pl.ds(HALO, tokens)], in_sem.at[0]),
        pltpu.make_async_copy(k_hbm, kvpad.at[0, pl.ds(HALO, tokens)], in_sem.at[1]),
        pltpu.make_async_copy(v_hbm, kvpad.at[1, pl.ds(HALO, tokens)], in_sem.at[2]),
    ]
    for n in (1, 2, 0):
        loads[n].start()

    barrier = pltpu.get_barrier_semaphore()
    for r in range(1, ni):
        pl.semaphore_signal(barrier, inc=1, device_id=inner_peer(r), device_id_type=MESH)
    for r in range(1, no):
        pl.semaphore_signal(
            barrier, inc=1, device_id={"outer": lax.rem(o + r, no)}, device_id_type=MESH
        )

    @pl.when(has_next)
    def _():
        pl.semaphore_signal(barrier, inc=1, device_id=chain(1), device_id_type=MESH)

    @pl.when(has_prev)
    def _():
        pl.semaphore_signal(barrier, inc=1, device_id=chain(-1), device_id_type=MESH)

    phase = jnp.int32(-1)
    for b in range(nb):
        for e in range(entries):
            entry = list_ref[b, e]
            distant = (entry >= 0) & (entry <= d * nb + b - LOCAL)
            phase = jnp.maximum(phase, jnp.where(distant, lax.rem(entry, STRIDE), -1))
    for b in range(nb):
        hit = lax.rem((d - 1) * nb + b + STRIDE, STRIDE) == phase
        wout[b : b + 1, :] = jnp.full((1, 128), jnp.where(hit, 1.0, 0.0), jnp.float32)
    if nb < wout.shape[0]:
        wout[nb:, :] = jnp.zeros((wout.shape[0] - nb, 128), jnp.float32)

    @pl.when(d == 0)
    def _():
        qpad[0:HALO, :] = jnp.zeros((HALO, qw), jnp.bfloat16)
        kvpad[:, 0:HALO, :] = jnp.zeros((2, HALO, kvw), jnp.bfloat16)
        kvc[:, 0:BLOCK, :] = jnp.zeros((2, BLOCK, kvw), jnp.bfloat16)

    @pl.when(d == last)
    def _():
        win[...] = jnp.zeros(win.shape, jnp.float32)

    fsum[...] = jnp.zeros(fsum.shape, jnp.bfloat16)

    pl.semaphore_wait(
        barrier,
        ni - 1 + no - 1 + jnp.where(has_next, 1, 0) + jnp.where(has_prev, 1, 0),
    )

    w_copy = pltpu.make_async_remote_copy(
        wout, win, w_s, w_r, device_id=chain(-1), device_id_type=MESH
    )
    rim = pl.ds(tokens - HALO, HALO)
    tails = [
        pltpu.make_async_remote_copy(
            src.at[rim], dst, tail_s.at[n], tail_r.at[n], device_id=chain(1), device_id_type=MESH
        )
        for n, (src, dst) in enumerate(
            (
                (k_hbm, kvpad.at[0, pl.ds(0, HALO)]),
                (v_hbm, kvpad.at[1, pl.ds(0, HALO)]),
                (q_hbm, qpad.at[pl.ds(0, HALO)]),
            )
        )
    ]
    window = pltpu.make_async_remote_copy(
        kvc.at[:, pl.ds(tokens, BLOCK)],
        kvc.at[:, pl.ds(0, BLOCK)],
        win_s,
        win_r,
        device_id=chain(1),
        device_id_type=MESH,
    )

    @pl.when(has_prev)
    def _():
        w_copy.start()

    @pl.when(has_next)
    def _():
        for copy in tails:
            copy.start()

    def kv_conv(b):
        rows = slice(b * BLOCK, b * BLOCK + BLOCK + HALO)
        dst = slice((b + 1) * BLOCK, (b + 2) * BLOCK)
        kvc[0, dst, :] = conv(kvpad[0, rows, :], kt_ref[...])
        kvc[1, dst, :] = conv(kvpad[1, rows, :], vt_ref[...])

    loads[1].wait()
    loads[2].wait()
    kv_conv(nb - 1)

    @pl.when(has_next)
    def _():
        window.start()

    for b in range(1, nb - 1):
        kv_conv(b)

    @pl.when(has_prev)
    def _():
        tails[0].wait_recv()
        tails[1].wait_recv()

    kv_conv(0)

    @pl.when(has_next)
    def _():
        w_copy.wait_recv()

    for g in range(groups):
        cols = slice(g * HEAD_DIM, (g + 1) * HEAD_DIM)
        for half in range(2):
            total = jnp.zeros((BLOCK, HEAD_DIM), jnp.float32)
            for b in range(nb):
                own = jnp.where(lax.rem(d * nb + b, STRIDE) == phase, 1.0, 0.0)
                weight = jnp.maximum(win[b : b + 1, :], own)
                rows = slice((b + 1) * BLOCK, (b + 2) * BLOCK)
                total = total + weight * kvc[half, rows, cols].astype(jnp.float32)
            cand[half * BLOCK : (half + 1) * BLOCK, cols] = total.astype(jnp.bfloat16)

    def part(index):
        return pl.ds(pl.multiple_of(index * piece, piece), piece)

    scatters = [
        pltpu.make_async_remote_copy(
            cand.at[part(lax.rem(i + r, ni))],
            rbuf.at[r],
            sc_s.at[r],
            sc_r.at[r],
            device_id=inner_peer(r),
            device_id_type=MESH,
        )
        for r in range(1, ni)
    ]
    columns = [
        pltpu.make_async_remote_copy(
            zpiece,
            zbuf.at[r],
            z_s.at[r],
            z_r.at[r],
            device_id={"outer": lax.rem(o + r, no)},
            device_id_type=MESH,
        )
        for r in range(1, no)
    ]
    gathers = [
        pltpu.make_async_remote_copy(
            fsum,
            far.at[:, part(i)],
            g_s.at[r],
            g_r.at[r],
            device_id=inner_peer(r),
            device_id_type=MESH,
        )
        for r in range(1, ni)
    ]
    for copy in scatters:
        copy.start()

    def column_step():
        total = cand[part(i), :].astype(jnp.float32)
        for n, copy in enumerate(scatters):
            copy.wait_recv()
            total = total + rbuf[n + 1].astype(jnp.float32)
        zpiece[...] = total.astype(jnp.bfloat16)
        for n, copy in enumerate(columns):
            pl.when(o + n + 1 < no)(copy.start)

    def slot_of(row):
        return lax.rem(row * (ni * nb) // STRIDE, slots)

    def gather_step():
        fsum[slot_of(o)] = zpiece[...]
        for n, copy in enumerate(columns):
            r = n + 1

            @pl.when(o >= r)
            def _():
                copy.wait_recv()
                at = slot_of(o - r)
                fsum[at] = (
                    fsum[at].astype(jnp.float32) + zbuf[r].astype(jnp.float32)
                ).astype(jnp.bfloat16)

        for copy in gathers:
            copy.start()
        far[:, part(i), :] = fsum[...]

    loads[0].wait()

    @pl.when(has_prev)
    def _():
        tails[2].wait_recv()

    row_ids = lax.broadcasted_iota(jnp.int32, (BLOCK, BLOCK), 0)
    col_ids = lax.broadcasted_iota(jnp.int32, (BLOCK, BLOCK), 1)
    causal = jnp.concatenate([row_ids >= col_ids] * per_group, 0)
    ones = jnp.ones((LOCAL * BLOCK, HEAD_DIM), jnp.bfloat16)

    def near(step, carry):
        b = lax.rem(step + 1, nb)

        @pl.when((b == 0) & has_prev)
        def _():
            window.wait_recv()

        bias = jnp.where((b == 0) & (d == 0), NEG, 0.0)
        base = pl.multiple_of(b * BLOCK, BLOCK)
        for g in range(groups):
            wide = slice(g * per_group * HEAD_DIM, (g + 1) * per_group * HEAD_DIM)
            cols = slice(g * HEAD_DIM, (g + 1) * HEAD_DIM)
            q = conv(qpad[pl.ds(base, BLOCK + HALO), wide], qt_ref[:, wide])
            q = jnp.concatenate(
                [q[:, h * HEAD_DIM : (h + 1) * HEAD_DIM] for h in range(per_group)], 0
            )
            qs[b, g] = q
            k = kvc[0, pl.ds(base, LOCAL * BLOCK), cols]
            v = kvc[1, pl.ds(base, LOCAL * BLOCK), cols]
            s = lax.dot_general(q, k, NT, preferred_element_type=jnp.float32)
            before = s[:, :BLOCK] + bias
            own = jnp.where(causal, s[:, BLOCK:], NEG)
            peak = jnp.max(jnp.maximum(before, own), axis=1, keepdims=True)
            p = jnp.concatenate(
                [jnp.exp2((before - peak) * SCALE), jnp.exp2((own - peak) * SCALE)], 1
            ).astype(jnp.bfloat16)
            acc_ref[b, g] = jnp.dot(
                p, jnp.concatenate([v, ones], 1), preferred_element_type=jnp.float32
            )
            max_ref[b, g] = jnp.broadcast_to(peak, (per_group * BLOCK, HEAD_DIM))

        pl.when(step == 0)(column_step)
        pl.when(step == 2)(gather_step)
        return carry

    lax.fori_loop(0, nb, near, 0)
    for copy in gathers:
        copy.wait_recv()

    def result(b):
        rows = pl.ds(pl.multiple_of(b * BLOCK, BLOCK), BLOCK)
        return pltpu.make_async_copy(outb.at[rows], out_hbm.at[rows], out_sem.at[b])

    def distant_part(b, carry):
        base = pl.multiple_of(b * BLOCK, BLOCK)
        biases = []
        for n in range(slots):
            seen = jnp.int32(0)
            for e in range(entries):
                entry = list_ref[b, e]
                hit = (entry >= n * STRIDE) & (entry < (n + 1) * STRIDE)
                hit = hit & (entry <= d * nb + b - LOCAL)
                seen = jnp.where(hit, 1, seen)
            biases.append(jnp.where(seen > 0, 0.0, NEG))
        for g in range(groups):
            cols = slice(g * HEAD_DIM, (g + 1) * HEAD_DIM)
            q = qs[b, g]
            near_peak = max_ref[b, g]
            scores = []
            top = None
            for n in range(slots):
                s = lax.dot_general(
                    q, far[n, 0:BLOCK, cols], NT, preferred_element_type=jnp.float32
                )
                s = s + biases[n]
                scores.append(s)
                top = s if top is None else jnp.maximum(top, s)
            peak = jnp.maximum(near_peak, jnp.max(top, axis=1, keepdims=True))
            both = acc_ref[b, g]
            shrink = jnp.exp2((near_peak - peak) * SCALE)
            total = both[:, :HEAD_DIM] * shrink
            count = both[:, HEAD_DIM:] * shrink
            for n in range(slots):
                p = jnp.exp2((scores[n] - peak) * SCALE).astype(jnp.bfloat16)
                more = jnp.dot(
                    p,
                    jnp.concatenate([far[n, BLOCK : 2 * BLOCK, cols], ones[:BLOCK]], 1),
                    preferred_element_type=jnp.float32,
                )
                total = total + more[:, :HEAD_DIM]
                count = count + more[:, HEAD_DIM:]
            mixed = (total / count).astype(jnp.bfloat16)
            for h in range(per_group):
                head = g * per_group + h
                outb[pl.ds(base, BLOCK), head * HEAD_DIM : (head + 1) * HEAD_DIM] = mixed[
                    h * BLOCK : (h + 1) * BLOCK
                ]
        result(b).start()
        return carry

    lax.fori_loop(0, nb, distant_part, 0)

    @pl.when(has_prev)
    def _():
        w_copy.wait_send()

    @pl.when(has_next)
    def _():
        for copy in tails:
            copy.wait_send()
        window.wait_send()

    for copy in scatters + gathers:
        copy.wait_send()
    for n, copy in enumerate(columns):
        pl.when(o + n + 1 < no)(copy.wait_send)
    for b in range(nb):
        result(b).wait()


def body(q_proj, k_proj, v_proj, q_taps, k_taps, v_taps, block_list):
    tokens, qw = q_proj.shape
    kvw = k_proj.shape[1]
    ni = lax.axis_size("inner")
    no = lax.axis_size("outer")
    nb = tokens // BLOCK
    groups = kvw // HEAD_DIM
    rows = qw // kvw * BLOCK
    slots = max(1, nb * ni * no // STRIDE)
    piece = 2 * BLOCK // ni
    dma = pltpu.SemaphoreType.DMA
    bf16, f32 = jnp.bfloat16, jnp.float32
    any_spec = pl.BlockSpec(memory_space=pl.ANY)
    vmem_spec = pl.BlockSpec(memory_space=pltpu.VMEM)
    scores = nb * groups * rows * (LOCAL + slots) * BLOCK
    return pl.pallas_call(
        functools.partial(kernel, ni, no),
        out_shape=jax.ShapeDtypeStruct((tokens, qw), bf16),
        in_specs=[pl.BlockSpec(memory_space=pltpu.SMEM)] + [any_spec] * 3 + [vmem_spec] * 3,
        out_specs=any_spec,
        scratch_shapes=[
            pltpu.VMEM((tokens + HALO, qw), bf16),
            pltpu.VMEM((2, tokens + HALO, kvw), bf16),
            pltpu.VMEM((2, tokens + BLOCK, kvw), bf16),
            pltpu.VMEM((nb, groups, rows, HEAD_DIM), bf16),
            pltpu.VMEM((nb, groups, rows, 2 * HEAD_DIM), f32),
            pltpu.VMEM((nb, groups, rows, HEAD_DIM), f32),
            pltpu.VMEM((tokens, qw), bf16),
            pltpu.VMEM((max(8, nb), 128), f32),
            pltpu.VMEM((max(8, nb), 128), f32),
            pltpu.VMEM((2 * BLOCK, kvw), bf16),
            pltpu.VMEM((ni, piece, kvw), bf16),
            pltpu.VMEM((piece, kvw), bf16),
            pltpu.VMEM((no, piece, kvw), bf16),
            pltpu.VMEM((slots, piece, kvw), bf16),
            pltpu.VMEM((slots, 2 * BLOCK, kvw), bf16),
            dma((3,)),
            dma((3,)),
            dma((3,)),
            dma,
            dma,
            dma,
            dma,
            dma((ni,)),
            dma((ni,)),
            dma((no,)),
            dma((no,)),
            dma((ni,)),
            dma((ni,)),
            dma((nb,)),
        ],
        compiler_params=pltpu.CompilerParams(
            collective_id=0, has_side_effects=True, vmem_limit_bytes=48 * 1024 * 1024
        ),
        cost_estimate=pl.CostEstimate(
            flops=4 * scores * HEAD_DIM,
            bytes_accessed=4 * tokens * qw + 4 * tokens * kvw,
            transcendentals=scores,
        ),
    )(block_list, q_proj, k_proj, v_proj, q_taps, k_taps, v_taps)


def solution(mesh):
    rows = P(("groups", "outer", "inner"), None)
    return jax.shard_map(
        body,
        mesh=mesh,
        in_specs=(rows, rows, rows, P(), P(), P(), rows),
        out_specs=rows,
        check_vma=False,
    )
```

time: 178 us -> 36.5 us (0.21)
  the two profiles are of different devices: /device:TPU:0 before, /device:TPU:29 now
where the time goes in v1:
time: 36.5 us; the launch traced here: 36.1 us
  Pallas kernels  28.2 us (77%)
  local copies, waits for them, and re-layouts  7.83 us (21%)
    pallas_call x1, Pallas kernels, body(): pl.pallas_call(functools.partial(kernel, ni, no), out_shape=jax.ShapeDtyp...  28.2 us
    unnamed x15, local copies, waits for them, and re-layouts  7.83 us

profile of v1, /device:TPU:29, one launch (start us, length us, event | category | flops | bytes accessed | tf_op | source)
XLA Modules:
  0.0 36.1 jit_solution(4048450856389501410)
XLA Ops:
  0.0 0.0 copy-start
  0.0 1.6 %copy-done = bf16[512,2048]{1,0:T(8,128)(2,1)S(1)} copy-done((bf16[512,2048]{1,0:T(8,128)(2,1)S(1)}, bf16[512,2048]{1,0:T(8,128)(2,1)}, u32[]{:S(2)}) %copy-start) | copy-done | bytes 2097176
  1.6 0.0 copy-start.1
  1.6 1.0 %copy-done.1 = bf16[512,512]{1,0:T(8,128)(2,1)S(1)} copy-done((bf16[512,512]{1,0:T(8,128)(2,1)S(1)}, bf16[512,512]{1,0:T(8,128)(2,1)}, u32[]{:S(2)}) %copy-start.1) | copy-done | bytes 524312
  2.6 0.0 copy-start.2
  2.6 1.0 %copy-done.2 = bf16[512,512]{1,0:T(8,128)(2,1)S(1)} copy-done((bf16[512,512]{1,0:T(8,128)(2,1)S(1)}, bf16[512,512]{1,0:T(8,128)(2,1)}, u32[]{:S(2)}) %copy-start.2) | copy-done | bytes 524312
  3.7 0.0 copy-start.3
  3.7 0.8 %copy-done.3 = f32[3,2048]{1,0:T(4,128)S(1)} copy-done((f32[3,2048]{1,0:T(4,128)S(1)}, f32[3,2048]{1,0:T(4,128)}, u32[]{:S(2)}) %copy-start.3) | copy-done | bytes 24600
  4.4 0.0 copy-start.4
  4.4 0.7 %copy-done.4 = f32[3,512]{1,0:T(4,128)S(1)} copy-done((f32[3,512]{1,0:T(4,128)S(1)}, f32[3,512]{1,0:T(4,128)}, u32[]{:S(2)}) %copy-start.4) | copy-done | bytes 6168
  5.1 0.0 copy-start.5
  5.1 0.7 %copy-done.5 = f32[3,512]{1,0:T(4,128)S(1)} copy-done((f32[3,512]{1,0:T(4,128)S(1)}, f32[3,512]{1,0:T(4,128)}, u32[]{:S(2)}) %copy-start.5) | copy-done | bytes 6168
  5.8 0.0 copy-start.6
  5.8 0.7 %copy-done.6 = s32[4,3]{1,0:T(4,128)S(1)} copy-done((s32[4,3]{1,0:T(4,128)S(1)}, s32[4,3]{1,0:T(4,128)}, u32[]{:S(2)}) %copy-start.6) | copy-done | bytes 72
  6.5 28.2 %shard_map.73 = bf16[512,2048]{1,0:T(8,128)(2,1)S(1)} custom-call(s32[4,3]{1,0:T(4,128)S(1)} %copy-done.6, bf16[512,2048]{1,0:T(8,128)(2,1)S(1)} %copy-done, bf16[512,512]{1,0:T(8,128)(2,1)S(1)} %copy-done.1, bf16[512,512]{1,0:T(8,128)(2,1)S(1)} %copy-done.2, f32[3,2048]{1,0:T(4,128)S(1)} %copy-done.3, f32[3,512]{1,0:T(4,128)S(1)} %copy-done.4, ...), custom_call_target="tpu_custom_call" | custom-call | flops 1610612736 | bytes 5242880 | tf_op jit(solution)/shard_map/pallas_call | solution.py:388
  34.7 1.3 %copy.9 = bf16[512,2048]{1,0:T(8,128)(2,1)} copy(bf16[512,2048]{1,0:T(8,128)(2,1)S(1)} %shard_map.73) | data formatting | bytes 4194304
Async XLA Ops:
  0.0 1.6 %copy-start = (bf16[512,2048]{1,0:T(8,128)(2,1)S(1)}, bf16[512,2048]{1,0:T(8,128)(2,1)}, u32[]{:S(2)}) copy-start(bf16[512,2048]{1,0:T(8,128)(2,1)} %q_hbm.1) | copy-start | bytes 6291460
  1.6 1.0 %copy-start.1 = (bf16[512,512]{1,0:T(8,128)(2,1)S(1)}, bf16[512,512]{1,0:T(8,128)(2,1)}, u32[]{:S(2)}) copy-start(bf16[512,512]{1,0:T(8,128)(2,1)} %k_hbm.1) | copy-start | bytes 1572868
  2.6 1.0 %copy-start.2 = (bf16[512,512]{1,0:T(8,128)(2,1)S(1)}, bf16[512,512]{1,0:T(8,128)(2,1)}, u32[]{:S(2)}) copy-start(bf16[512,512]{1,0:T(8,128)(2,1)} %v_hbm.1) | copy-start | bytes 1572868
  3.7 0.8 %copy-start.3 = (f32[3,2048]{1,0:T(4,128)S(1)}, f32[3,2048]{1,0:T(4,128)}, u32[]{:S(2)}) copy-start(f32[3,2048]{1,0:T(4,128)} %qt_ref.1) | copy-start | bytes 73732
  4.4 0.7 %copy-start.4 = (f32[3,512]{1,0:T(4,128)S(1)}, f32[3,512]{1,0:T(4,128)}, u32[]{:S(2)}) copy-start(f32[3,512]{1,0:T(4,128)} %kt_ref.1) | copy-start | bytes 18436
  5.1 0.7 %copy-start.5 = (f32[3,512]{1,0:T(4,128)S(1)}, f32[3,512]{1,0:T(4,128)}, u32[]{:S(2)}) copy-start(f32[3,512]{1,0:T(4,128)} %vt_ref.1) | copy-start | bytes 18436
  5.8 0.7 %copy-start.6 = (s32[4,3]{1,0:T(4,128)S(1)}, s32[4,3]{1,0:T(4,128)}, u32[]{:S(2)}) copy-start(s32[4,3]{1,0:T(4,128)} %list_ref.1) | copy-start | bytes 148

commit v2 on v1

v2 whole, which is shorter than its diff:
```python
import functools
import math

import jax
import jax.numpy as jnp
from jax import lax
from jax.experimental import pallas as pl
from jax.experimental.pallas import tpu as pltpu
from jax.sharding import PartitionSpec as P

HEAD_DIM = 128
BLOCK = 128
LOCAL = 2
STRIDE = 64
HALO = 16
NEG = -1e30
MESH = pl.DeviceIdType.MESH
SCALE = math.log2(math.e) / math.sqrt(HEAD_DIM)
NT = (((1,), (1,)), ((), ()))


def conv(padded, taps):
    wide = padded.astype(jnp.float32)
    total = taps[0:1] * wide[HALO:]
    for j in (1, 2):
        total = total + taps[j : j + 1] * pltpu.roll(wide, j, 0)[HALO:]
    return total.astype(jnp.bfloat16)


def kernel(
    ni, no, list_hbm, q_hbm, k_hbm, v_hbm, qt_hbm, kt_hbm, vt_hbm, out_hbm,
    list_ref, qt_ref, kt_ref, vt_ref, qpad, kvpad, kvc, qs, acc_ref, max_ref, pbuf, outb, wout, win, cand, rbuf, zpiece, zbuf,
    fsum, far, in_sem, tail_s, tail_r, w_s, w_r, sc_s, sc_r, z_s, z_r,
    g_s, g_r, out_sem,
):
    tokens, qw = q_hbm.shape
    kvw = k_hbm.shape[1]
    groups = kvw // HEAD_DIM
    per_group = qw // kvw
    nb = tokens // BLOCK
    slots = far.shape[1]
    piece_rows, piece_cols = zpiece.shape[1:]
    col_parts = kvw // piece_cols
    before = BLOCK + HALO
    entries = list_ref.shape[1]
    o = lax.axis_index("outer")
    i = lax.axis_index("inner")
    d = o * ni + i
    last = ni * no - 1
    has_next = d < last
    has_prev = d > 0

    def chain(step):
        other = d + step
        return {"outer": other // ni, "inner": lax.rem(other, ni)}

    def inner_peer(r):
        return {"inner": lax.rem(i + r, ni)}

    loads = [
        pltpu.make_async_copy(q_hbm, qpad.at[pl.ds(HALO, tokens)], in_sem.at[0]),
        pltpu.make_async_copy(k_hbm, kvpad.at[0, pl.ds(before, tokens)], in_sem.at[1]),
        pltpu.make_async_copy(v_hbm, kvpad.at[1, pl.ds(before, tokens)], in_sem.at[2]),
        pltpu.make_async_copy(list_hbm, list_ref, in_sem.at[3]),
        pltpu.make_async_copy(qt_hbm, qt_ref, in_sem.at[4]),
        pltpu.make_async_copy(kt_hbm, kt_ref, in_sem.at[5]),
        pltpu.make_async_copy(vt_hbm, vt_ref, in_sem.at[6]),
    ]
    for n in (3, 1, 5, 2, 6, 0, 4):
        loads[n].start()

    barrier = pltpu.get_barrier_semaphore()
    for r in range(1, ni):
        pl.semaphore_signal(barrier, inc=1, device_id=inner_peer(r), device_id_type=MESH)
    for r in range(1, no):
        pl.semaphore_signal(
            barrier, inc=1, device_id={"outer": lax.rem(o + r, no)}, device_id_type=MESH
        )

    @pl.when(has_next)
    def _():
        pl.semaphore_signal(barrier, inc=1, device_id=chain(1), device_id_type=MESH)

    @pl.when(has_prev)
    def _():
        pl.semaphore_signal(barrier, inc=1, device_id=chain(-1), device_id_type=MESH)

    loads[3].wait()
    phase = jnp.int32(-1)
    for b in range(nb):
        for e in range(entries):
            entry = list_ref[b, e]
            distant = (entry >= 0) & (entry <= d * nb + b - LOCAL)
            phase = jnp.maximum(phase, jnp.where(distant, lax.rem(entry, STRIDE), -1))
    for b in range(nb):
        hit = lax.rem((d - 1) * nb + b + STRIDE, STRIDE) == phase
        wout[b : b + 1, :] = jnp.full((1, 128), jnp.where(hit, 1.0, 0.0), jnp.float32)
    if nb < wout.shape[0]:
        wout[nb:, :] = jnp.zeros((wout.shape[0] - nb, 128), jnp.float32)

    @pl.when(d == 0)
    def _():
        qpad[0:HALO, :] = jnp.zeros((HALO, qw), jnp.bfloat16)
        kvpad[:, 0:before, :] = jnp.zeros((2, before, kvw), jnp.bfloat16)

    @pl.when(d == last)
    def _():
        win[...] = jnp.zeros(win.shape, jnp.float32)

    fsum[...] = jnp.zeros(fsum.shape, jnp.bfloat16)

    pl.semaphore_wait(
        barrier,
        ni - 1 + no - 1 + jnp.where(has_next, 1, 0) + jnp.where(has_prev, 1, 0),
    )

    w_copy = pltpu.make_async_remote_copy(
        wout, win, w_s, w_r, device_id=chain(-1), device_id_type=MESH
    )
    rim = pl.ds(tokens - HALO, HALO)
    body_rows = pl.ds(tokens - before, BLOCK)

    def to_next(src, dst, n):
        return pltpu.make_async_remote_copy(
            src, dst, tail_s.at[n], tail_r.at[n], device_id=chain(1), device_id_type=MESH
        )

    tails = [
        to_next(k_hbm.at[rim], kvpad.at[0, pl.ds(BLOCK, HALO)], 0),
        to_next(v_hbm.at[rim], kvpad.at[1, pl.ds(BLOCK, HALO)], 1),
        to_next(k_hbm.at[body_rows], kvpad.at[0, pl.ds(0, BLOCK)], 2),
        to_next(v_hbm.at[body_rows], kvpad.at[1, pl.ds(0, BLOCK)], 3),
        to_next(q_hbm.at[rim], qpad.at[pl.ds(0, HALO)], 4),
    ]

    @pl.when(has_prev)
    def _():
        w_copy.start()

    @pl.when(has_next)
    def _():
        for copy in tails:
            copy.start()

    def kv_conv(b):
        rows = slice(b * BLOCK, b * BLOCK + before)
        dst = slice(b * BLOCK, (b + 1) * BLOCK)
        kvc[0, dst, :] = conv(kvpad[0, rows, :], kt_ref[...])
        kvc[1, dst, :] = conv(kvpad[1, rows, :], vt_ref[...])

    for n in (1, 5, 2, 6):
        loads[n].wait()
    for b in range(2, nb + 1):
        kv_conv(b)

    @pl.when(has_prev)
    def _():
        tails[0].wait_recv()
        tails[1].wait_recv()

    kv_conv(1)

    @pl.when(has_next)
    def _():
        w_copy.wait_recv()

    for g in range(groups):
        cols = slice(g * HEAD_DIM, (g + 1) * HEAD_DIM)
        for half in range(2):
            total = jnp.zeros((BLOCK, HEAD_DIM), jnp.float32)
            for b in range(nb):
                own = jnp.where(lax.rem(d * nb + b, STRIDE) == phase, 1.0, 0.0)
                weight = jnp.maximum(win[b : b + 1, :], own)
                rows = slice((b + 1) * BLOCK, (b + 2) * BLOCK)
                total = total + weight * kvc[half, rows, cols].astype(jnp.float32)
            cand[half, :, cols] = total.astype(jnp.bfloat16)

    def part(index):
        row = pl.multiple_of(index // col_parts * piece_rows, piece_rows)
        col = pl.multiple_of(lax.rem(index, col_parts) * piece_cols, piece_cols)
        return pl.ds(row, piece_rows), pl.ds(col, piece_cols)

    def scatter(half, r):
        return pltpu.make_async_remote_copy(
            cand.at[(half, *part(lax.rem(i + r, ni)))],
            rbuf.at[half, r],
            sc_s.at[half, r],
            sc_r.at[half, r],
            device_id=inner_peer(r),
            device_id_type=MESH,
        )

    def column(half, r):
        return pltpu.make_async_remote_copy(
            zpiece.at[half],
            zbuf.at[half, r],
            z_s.at[half, r],
            z_r.at[half, r],
            device_id={"outer": lax.rem(o + r, no)},
            device_id_type=MESH,
        )

    def gather(half, r):
        return pltpu.make_async_remote_copy(
            fsum.at[half],
            far.at[(half, slice(None), *part(i))],
            g_s.at[half, r],
            g_r.at[half, r],
            device_id=inner_peer(r),
            device_id_type=MESH,
        )

    for half in range(2):
        for r in range(1, ni):
            scatter(half, r).start()

    def column_step(half):
        total = cand[(half, *part(i))].astype(jnp.float32)
        for r in range(1, ni):
            scatter(half, r).wait_recv()
            total = total + rbuf[half, r].astype(jnp.float32)
        zpiece[half] = total.astype(jnp.bfloat16)
        for r in range(1, no):
            pl.when(o + r < no)(column(half, r).start)

    def slot_of(row):
        return lax.rem(row * (ni * nb) // STRIDE, slots)

    def gather_step(half):
        fsum[half, slot_of(o)] = zpiece[half]
        for r in range(1, no):

            @pl.when(o >= r)
            def _():
                column(half, r).wait_recv()
                at = slot_of(o - r)
                fsum[half, at] = (
                    fsum[half, at].astype(jnp.float32) + zbuf[half, r].astype(jnp.float32)
                ).astype(jnp.bfloat16)

        for r in range(1, ni):
            gather(half, r).start()
        far[(half, slice(None), *part(i))] = fsum[half]

    def gather_wait(half):
        for r in range(1, ni):
            gather(half, r).wait_recv()

    loads[0].wait()
    loads[4].wait()

    @pl.when(has_prev)
    def _():
        tails[4].wait_recv()

    row_ids = lax.broadcasted_iota(jnp.int32, (BLOCK, BLOCK), 0)
    col_ids = lax.broadcasted_iota(jnp.int32, (BLOCK, BLOCK), 1)
    causal = jnp.concatenate([row_ids >= col_ids] * per_group, 0)
    ones = jnp.ones((LOCAL * BLOCK, HEAD_DIM), jnp.bfloat16)

    def near(step, carry):
        b = lax.rem(step + 1, nb)

        @pl.when(b == 0)
        def _():
            @pl.when(has_prev)
            def _():
                tails[2].wait_recv()
                tails[3].wait_recv()

            kv_conv(0)

        bias = jnp.where((b == 0) & (d == 0), NEG, 0.0)
        base = pl.multiple_of(b * BLOCK, BLOCK)
        for g in range(groups):
            wide = slice(g * per_group * HEAD_DIM, (g + 1) * per_group * HEAD_DIM)
            cols = slice(g * HEAD_DIM, (g + 1) * HEAD_DIM)
            q = conv(qpad[pl.ds(base, BLOCK + HALO), wide], qt_ref[:, wide])
            q = jnp.concatenate(
                [q[:, h * HEAD_DIM : (h + 1) * HEAD_DIM] for h in range(per_group)], 0
            )
            qs[b, g] = q
            k = kvc[0, pl.ds(base, LOCAL * BLOCK), cols]
            v = kvc[1, pl.ds(base, LOCAL * BLOCK), cols]
            s = lax.dot_general(q, k, NT, preferred_element_type=jnp.float32)
            prev = s[:, :BLOCK] + bias
            own = jnp.where(causal, s[:, BLOCK:], NEG)
            peak = jnp.max(jnp.maximum(prev, own), axis=1, keepdims=True)
            p = jnp.concatenate(
                [jnp.exp2((prev - peak) * SCALE), jnp.exp2((own - peak) * SCALE)], 1
            ).astype(jnp.bfloat16)
            acc_ref[b, g] = jnp.dot(
                p, jnp.concatenate([v, ones], 1), preferred_element_type=jnp.float32
            )
            max_ref[b, g] = jnp.broadcast_to(peak, (per_group * BLOCK, HEAD_DIM))

        @pl.when(step == 1)
        def _():
            column_step(0)
            column_step(1)

        return carry

    lax.fori_loop(0, nb, near, 0)
    gather_step(0)
    gather_step(1)
    gather_wait(0)

    def result(b):
        rows = pl.ds(pl.multiple_of(b * BLOCK, BLOCK), BLOCK)
        return pltpu.make_async_copy(outb.at[rows], out_hbm.at[rows], out_sem.at[b])

    def distant_keys(b, carry):
        biases = []
        for n in range(slots):
            seen = jnp.int32(0)
            for e in range(entries):
                entry = list_ref[b, e]
                hit = (entry >= n * STRIDE) & (entry < (n + 1) * STRIDE)
                hit = hit & (entry <= d * nb + b - LOCAL)
                seen = jnp.where(hit, 1, seen)
            biases.append(jnp.where(seen > 0, 0.0, NEG))
        for g in range(groups):
            cols = slice(g * HEAD_DIM, (g + 1) * HEAD_DIM)
            q = qs[b, g]
            near_peak = max_ref[b, g]
            scores = []
            top = None
            for n in range(slots):
                s = lax.dot_general(q, far[0, n, :, cols], NT, preferred_element_type=jnp.float32)
                s = s + biases[n]
                scores.append(s)
                top = s if top is None else jnp.maximum(top, s)
            peak = jnp.maximum(near_peak, jnp.max(top, axis=1, keepdims=True))
            max_ref[b, g] = jnp.exp2((near_peak - peak) * SCALE)
            for n in range(slots):
                p = jnp.exp2((scores[n] - peak) * SCALE)
                pbuf[b, g, :, n * BLOCK : (n + 1) * BLOCK] = p.astype(jnp.bfloat16)
        return carry

    def distant_values(b, carry):
        base = pl.multiple_of(b * BLOCK, BLOCK)
        for g in range(groups):
            cols = slice(g * HEAD_DIM, (g + 1) * HEAD_DIM)
            both = acc_ref[b, g]
            shrink = max_ref[b, g]
            total = both[:, :HEAD_DIM] * shrink
            count = both[:, HEAD_DIM:] * shrink
            for n in range(slots):
                more = jnp.dot(
                    pbuf[b, g, :, n * BLOCK : (n + 1) * BLOCK],
                    jnp.concatenate([far[1, n, :, cols], ones[:BLOCK]], 1),
                    preferred_element_type=jnp.float32,
                )
                total = total + more[:, :HEAD_DIM]
                count = count + more[:, HEAD_DIM:]
            mixed = (total / count).astype(jnp.bfloat16)
            for h in range(per_group):
                head = g * per_group + h
                outb[pl.ds(base, BLOCK), head * HEAD_DIM : (head + 1) * HEAD_DIM] = mixed[
                    h * BLOCK : (h + 1) * BLOCK
                ]
        result(b).start()
        return carry

    lax.fori_loop(0, nb, distant_keys, 0)
    gather_wait(1)
    lax.fori_loop(0, nb, distant_values, 0)

    @pl.when(has_prev)
    def _():
        w_copy.wait_send()

    @pl.when(has_next)
    def _():
        for copy in tails:
            copy.wait_send()

    for half in range(2):
        for r in range(1, ni):
            scatter(half, r).wait_send()
            gather(half, r).wait_send()
        for r in range(1, no):
            pl.when(o + r < no)(column(half, r).wait_send)
    for b in range(nb):
        result(b).wait()


def body(q_proj, k_proj, v_proj, q_taps, k_taps, v_taps, block_list):
    tokens, qw = q_proj.shape
    kvw = k_proj.shape[1]
    ni = lax.axis_size("inner")
    no = lax.axis_size("outer")
    nb = tokens // BLOCK
    groups = kvw // HEAD_DIM
    rows = qw // kvw * BLOCK
    slots = max(1, nb * ni * no // STRIDE)
    piece_rows = max(HALO, BLOCK // ni)
    piece_cols = BLOCK * kvw // (ni * piece_rows)
    piece = (piece_rows, piece_cols)
    dma = pltpu.SemaphoreType.DMA
    bf16, f32 = jnp.bfloat16, jnp.float32
    hbm_spec = pl.BlockSpec(memory_space=pltpu.HBM)
    scores = nb * groups * rows * (LOCAL + slots) * BLOCK
    return pl.pallas_call(
        functools.partial(kernel, ni, no),
        out_shape=jax.ShapeDtypeStruct((tokens, qw), bf16),
        in_specs=[hbm_spec] * 7,
        out_specs=hbm_spec,
        scratch_shapes=[
            pltpu.SMEM(block_list.shape, jnp.int32),
            pltpu.VMEM(q_taps.shape, f32),
            pltpu.VMEM(k_taps.shape, f32),
            pltpu.VMEM(v_taps.shape, f32),
            pltpu.VMEM((tokens + HALO, qw), bf16),
            pltpu.VMEM((2, tokens + BLOCK + HALO, kvw), bf16),
            pltpu.VMEM((2, tokens + BLOCK, kvw), bf16),
            pltpu.VMEM((nb, groups, rows, HEAD_DIM), bf16),
            pltpu.VMEM((nb, groups, rows, 2 * HEAD_DIM), f32),
            pltpu.VMEM((nb, groups, rows, HEAD_DIM), f32),
            pltpu.VMEM((nb, groups, rows, slots * BLOCK), bf16),
            pltpu.VMEM((tokens, qw), bf16),
            pltpu.VMEM((max(8, nb), 128), f32),
            pltpu.VMEM((max(8, nb), 128), f32),
            pltpu.VMEM((2, BLOCK, kvw), bf16),
            pltpu.VMEM((2, ni, *piece), bf16),
            pltpu.VMEM((2, *piece), bf16),
            pltpu.VMEM((2, no, *piece), bf16),
            pltpu.VMEM((2, slots, *piece), bf16),
            pltpu.VMEM((2, slots, BLOCK, kvw), bf16),
            dma((7,)),
            dma((5,)),
            dma((5,)),
            dma,
            dma,
            dma((2, ni)),
            dma((2, ni)),
            dma((2, no)),
            dma((2, no)),
            dma((2, ni)),
            dma((2, ni)),
            dma((nb,)),
        ],
        compiler_params=pltpu.CompilerParams(
            collective_id=0, has_side_effects=True, vmem_limit_bytes=64 * 1024 * 1024
        ),
        cost_estimate=pl.CostEstimate(
            flops=4 * scores * HEAD_DIM,
            bytes_accessed=4 * tokens * qw + 4 * tokens * kvw,
            transcendentals=scores,
        ),
    )(block_list, q_proj, k_proj, v_proj, q_taps, k_taps, v_taps)


def solution(mesh):
    rows = P(("groups", "outer", "inner"), None)
    return jax.shard_map(
        body,
        mesh=mesh,
        in_specs=(rows, rows, rows, P(), P(), P(), rows),
        out_specs=rows,
        check_vma=False,
    )
```

time: 36.5 us -> 28.1 us (0.77)
  local copies, waits for them, and re-layouts: 7.83 us -> 3.16 us
  Pallas kernels: 28.2 us -> 24.8 us
    unnamed x15 -> x1, local copies, waits for them, and re-layouts: 7.83 us -> 3.16 us
    pallas_call x1, Pallas kernels: 28.2 us -> 24.8 us  [body(): pl.pallas_call(functools.partial(kernel, ni, no), out_shape=jax.ShapeDtyp...]
where the time goes in v2:
time: 28.1 us; the launch traced here: 28 us
  Pallas kernels  24.8 us (88%)
  local copies, waits for them, and re-layouts  3.16 us (11%)
    pallas_call x1, Pallas kernels, body(): pl.pallas_call(functools.partial(kernel, ni, no), out_shape=jax.ShapeDtyp...  24.8 us
    unnamed x1, local copies, waits for them, and re-layouts  3.16 us

profile of v2, /device:TPU:29, one launch (start us, length us, event | category | flops | bytes accessed | tf_op | source)
XLA Modules:
  0.0 28.0 jit_solution(17103204093829131828)
XLA Ops:
  0.0 24.8 %shard_map.73 = bf16[512,2048]{1,0:T(8,128)(2,1)} custom-call(s32[4,3]{1,0:T(4,128)} %list_hbm.1, bf16[512,2048]{1,0:T(8,128)(2,1)} %q_hbm.1, bf16[512,512]{1,0:T(8,128)(2,1)} %k_hbm.1, bf16[512,512]{1,0:T(8,128)(2,1)} %v_hbm.1, f32[3,2048]{1,0:T(4,128)} %qt_hbm.1, f32[3,512]{1,0:T(4,128)} %kt_hbm.1, f32[3,512]{1,0:T(4,128)} %vt_hbm.1), custom_call_target="tpu_custom_call" | custom-call | flops 1610612736 | bytes 5242880 | tf_op jit(solution)/shard_map/pallas_call | solution.py:405
  24.8 3.2 %copy.9 = bf16[512,2048]{1,0:T(8,128)(2,1)} copy(bf16[512,2048]{1,0:T(8,128)(2,1)} %shard_map.73) | data formatting | bytes 4194304

commit v3 on v2

--- a/solution.py
+++ b/solution.py
@@ -109,11 +109,6 @@
 
     fsum[...] = jnp.zeros(fsum.shape, jnp.bfloat16)
 
-    pl.semaphore_wait(
-        barrier,
-        ni - 1 + no - 1 + jnp.where(has_next, 1, 0) + jnp.where(has_prev, 1, 0),
-    )
-
     w_copy = pltpu.make_async_remote_copy(
         wout, win, w_s, w_r, device_id=chain(-1), device_id_type=MESH
     )
@@ -133,14 +128,20 @@
         to_next(q_hbm.at[rim], qpad.at[pl.ds(0, HALO)], 4),
     ]
 
-    @pl.when(has_prev)
-    def _():
-        w_copy.start()
-
-    @pl.when(has_next)
-    def _():
-        for copy in tails:
-            copy.start()
+    def first_sends():
+        pl.semaphore_wait(
+            barrier,
+            ni - 1 + no - 1 + jnp.where(has_next, 1, 0) + jnp.where(has_prev, 1, 0),
+        )
+
+        @pl.when(has_prev)
+        def _():
+            w_copy.start()
+
+        @pl.when(has_next)
+        def _():
+            for copy in tails:
+                copy.start()
 
     def kv_conv(b):
         rows = slice(b * BLOCK, b * BLOCK + before)
@@ -153,27 +154,32 @@
     for b in range(2, nb + 1):
         kv_conv(b)
 
-    @pl.when(has_prev)
-    def _():
-        tails[0].wait_recv()
-        tails[1].wait_recv()
-
-    kv_conv(1)
-
-    @pl.when(has_next)
-    def _():
-        w_copy.wait_recv()
-
-    for g in range(groups):
-        cols = slice(g * HEAD_DIM, (g + 1) * HEAD_DIM)
+    def candidate_step():
+        @pl.when(has_prev)
+        def _():
+            tails[0].wait_recv()
+            tails[1].wait_recv()
+
+        kv_conv(1)
+
+        @pl.when(has_next)
+        def _():
+            w_copy.wait_recv()
+
+        for g in range(groups):
+            cols = slice(g * HEAD_DIM, (g + 1) * HEAD_DIM)
+            for half in range(2):
+                total = jnp.zeros((BLOCK, HEAD_DIM), jnp.float32)
+                for b in range(nb):
+                    own = jnp.where(lax.rem(d * nb + b, STRIDE) == phase, 1.0, 0.0)
+                    weight = jnp.maximum(win[b : b + 1, :], own)
+                    rows = slice((b + 1) * BLOCK, (b + 2) * BLOCK)
+                    total = total + weight * kvc[half, rows, cols].astype(jnp.float32)
+                cand[half, :, cols] = total.astype(jnp.bfloat16)
+
         for half in range(2):
-            total = jnp.zeros((BLOCK, HEAD_DIM), jnp.float32)
-            for b in range(nb):
-                own = jnp.where(lax.rem(d * nb + b, STRIDE) == phase, 1.0, 0.0)
-                weight = jnp.maximum(win[b : b + 1, :], own)
-                rows = slice((b + 1) * BLOCK, (b + 2) * BLOCK)
-                total = total + weight * kvc[half, rows, cols].astype(jnp.float32)
-            cand[half, :, cols] = total.astype(jnp.bfloat16)
+            for r in range(1, ni):
+                scatter(half, r).start()
 
     def part(index):
         row = pl.multiple_of(index // col_parts * piece_rows, piece_rows)
@@ -210,10 +216,6 @@
             device_id_type=MESH,
         )
 
-    for half in range(2):
-        for r in range(1, ni):
-            scatter(half, r).start()
-
     def column_step(half):
         total = cand[(half, *part(i))].astype(jnp.float32)
         for r in range(1, ni):
@@ -249,17 +251,13 @@
     loads[0].wait()
     loads[4].wait()
 
-    @pl.when(has_prev)
-    def _():
-        tails[4].wait_recv()
-
     row_ids = lax.broadcasted_iota(jnp.int32, (BLOCK, BLOCK), 0)
     col_ids = lax.broadcasted_iota(jnp.int32, (BLOCK, BLOCK), 1)
     causal = jnp.concatenate([row_ids >= col_ids] * per_group, 0)
     ones = jnp.ones((LOCAL * BLOCK, HEAD_DIM), jnp.bfloat16)
 
     def near(step, carry):
-        b = lax.rem(step + 1, nb)
+        b = jnp.where(step < nb - 2, step + 2, nb - 1 - step)
 
         @pl.when(b == 0)
         def _():
@@ -267,6 +265,7 @@
             def _():
                 tails[2].wait_recv()
                 tails[3].wait_recv()
+                tails[4].wait_recv()
 
             kv_conv(0)
 
@@ -294,7 +293,10 @@
             )
             max_ref[b, g] = jnp.broadcast_to(peak, (per_group * BLOCK, HEAD_DIM))
 
-        @pl.when(step == 1)
+        pl.when(step == 0)(first_sends)
+        pl.when(step == 1)(candidate_step)
+
+        @pl.when(step == 2)
         def _():
             column_step(0)
             column_step(1)

time: 28.1 us -> 27.5 us (0.979)
  Pallas kernels: 24.8 us -> 24.2 us
    pallas_call x1, Pallas kernels: 24.8 us -> 24.2 us  [body(): pl.pallas_call(functools.partial(kernel, ni, no), out_shape=jax.ShapeDtyp...]
where the time goes in v3:
time: 27.5 us; the launch traced here: 27.3 us
  Pallas kernels  24.2 us (88%)
  local copies, waits for them, and re-layouts  3.16 us (11%)
    pallas_call x1, Pallas kernels, body(): pl.pallas_call(functools.partial(kernel, ni, no), out_shape=jax.ShapeDtyp...  24.2 us
    unnamed x1, local copies, waits for them, and re-layouts  3.16 us

profile of v3, /device:TPU:29, one launch (start us, length us, event | category | flops | bytes accessed | tf_op | source)
XLA Modules:
  0.0 27.3 jit_solution(2416369190625099934)
XLA Ops:
  0.0 24.2 %shard_map.73 = bf16[512,2048]{1,0:T(8,128)(2,1)} custom-call(s32[4,3]{1,0:T(4,128)} %list_hbm.1, bf16[512,2048]{1,0:T(8,128)(2,1)} %q_hbm.1, bf16[512,512]{1,0:T(8,128)(2,1)} %k_hbm.1, bf16[512,512]{1,0:T(8,128)(2,1)} %v_hbm.1, f32[3,2048]{1,0:T(4,128)} %qt_hbm.1, f32[3,512]{1,0:T(4,128)} %kt_hbm.1, f32[3,512]{1,0:T(4,128)} %vt_hbm.1), custom_call_target="tpu_custom_call" | custom-call | flops 1610612736 | bytes 5242880 | tf_op jit(solution)/shard_map/pallas_call | solution.py:407
  24.2 3.2 %copy.9 = bf16[512,2048]{1,0:T(8,128)(2,1)} copy(bf16[512,2048]{1,0:T(8,128)(2,1)} %shard_map.73) | data formatting | bytes 4194304

commit v4 on v3

--- a/solution.py
+++ b/solution.py
@@ -28,10 +28,10 @@
 
 
 def kernel(
-    ni, no, list_hbm, q_hbm, k_hbm, v_hbm, qt_hbm, kt_hbm, vt_hbm, out_hbm,
-    list_ref, qt_ref, kt_ref, vt_ref, qpad, kvpad, kvc, qs, acc_ref, max_ref, pbuf, outb, wout, win, cand, rbuf, zpiece, zbuf,
+    ni, no, list_hbm, q_hbm, k_hbm, v_hbm, qt_hbm, kt_hbm, vt_hbm, outb,
+    list_ref, qt_ref, kt_ref, vt_ref, qpad, kvpad, kvc, qs, acc_ref, max_ref, pbuf, wout, win, cand, rbuf, zpiece, zbuf,
     fsum, far, in_sem, tail_s, tail_r, w_s, w_r, sc_s, sc_r, z_s, z_r,
-    g_s, g_r, out_sem,
+    g_s, g_r,
 ):
     tokens, qw = q_hbm.shape
     kvw = k_hbm.shape[1]
@@ -307,10 +307,6 @@
     gather_step(0)
     gather_step(1)
     gather_wait(0)
-
-    def result(b):
-        rows = pl.ds(pl.multiple_of(b * BLOCK, BLOCK), BLOCK)
-        return pltpu.make_async_copy(outb.at[rows], out_hbm.at[rows], out_sem.at[b])
 
     def distant_keys(b, carry):
         biases = []
@@ -362,7 +358,6 @@
                 outb[pl.ds(base, BLOCK), head * HEAD_DIM : (head + 1) * HEAD_DIM] = mixed[
                     h * BLOCK : (h + 1) * BLOCK
                 ]
-        result(b).start()
         return carry
 
     lax.fori_loop(0, nb, distant_keys, 0)
@@ -384,8 +379,6 @@
             gather(half, r).wait_send()
         for r in range(1, no):
             pl.when(o + r < no)(column(half, r).wait_send)
-    for b in range(nb):
-        result(b).wait()
 
 
 def body(q_proj, k_proj, v_proj, q_taps, k_taps, v_taps, block_list):
@@ -408,7 +401,7 @@
         functools.partial(kernel, ni, no),
         out_shape=jax.ShapeDtypeStruct((tokens, qw), bf16),
         in_specs=[hbm_spec] * 7,
-        out_specs=hbm_spec,
+        out_specs=pl.BlockSpec(memory_space=pltpu.VMEM),
         scratch_shapes=[
             pltpu.SMEM(block_list.shape, jnp.int32),
             pltpu.VMEM(q_taps.shape, f32),
@@ -421,7 +414,6 @@
             pltpu.VMEM((nb, groups, rows, 2 * HEAD_DIM), f32),
             pltpu.VMEM((nb, groups, rows, HEAD_DIM), f32),
             pltpu.VMEM((nb, groups, rows, slots * BLOCK), bf16),
-            pltpu.VMEM((tokens, qw), bf16),
             pltpu.VMEM((max(8, nb), 128), f32),
             pltpu.VMEM((max(8, nb), 128), f32),
             pltpu.VMEM((2, BLOCK, kvw), bf16),
@@ -441,17 +433,16 @@
             dma((2, no)),
             dma((2, ni)),
             dma((2, ni)),
-            dma((nb,)),
         ],
         compiler_params=pltpu.CompilerParams(
-            collective_id=0, has_side_effects=True, vmem_limit_bytes=64 * 1024 * 1024
+            collective_id=0, has_side_effects=True, vmem_limit_bytes=48 * 1024 * 1024
         ),
         cost_estimate=pl.CostEstimate(
             flops=4 * scores * HEAD_DIM,
             bytes_accessed=4 * tokens * qw + 4 * tokens * kvw,
             transcendentals=scores,
         ),
-    )(block_list, q_proj, k_proj, v_proj, q_taps, k_taps, v_taps)
+    )(*[pltpu.with_memory_space_constraint(x, pltpu.HBM) for x in (block_list, q_proj, k_proj, v_proj, q_taps, k_taps, v_taps)])
 
 
 def solution(mesh):

time: 27.5 us -> 24.8 us (0.902)
  local copies, waits for them, and re-layouts: 3.16 us -> 1.32 us
  Pallas kernels: 24.2 us -> 23.3 us
    unnamed x1, local copies, waits for them, and re-layouts: 3.16 us -> 1.32 us
    pallas_call x1, Pallas kernels: 24.2 us -> 23.3 us  [body(): pl.pallas_call(functools.partial(kernel, ni, no), out_shape=jax.ShapeDtyp...]
where the time goes in v4:
time: 24.8 us; the launch traced here: 24.7 us
  Pallas kernels  23.3 us (94%)
  local copies, waits for them, and re-layouts  1.32 us (5%)
    pallas_call x1, Pallas kernels, body(): pl.pallas_call(functools.partial(kernel, ni, no), out_shape=jax.ShapeDtyp...  23.3 us
    unnamed x1, local copies, waits for them, and re-layouts  1.32 us

profile of v4, /device:TPU:29, one launch (start us, length us, event | category | flops | bytes accessed | tf_op | source)
XLA Modules:
  0.0 24.7 jit_solution(5241176741107211604)
XLA Ops:
  0.0 23.3 %shard_map.73 = bf16[512,2048]{1,0:T(8,128)(2,1)S(1)} custom-call(s32[4,3]{1,0:T(4,128)} %list_hbm.1, bf16[512,2048]{1,0:T(8,128)(2,1)} %q_hbm.1, bf16[512,512]{1,0:T(8,128)(2,1)} %k_hbm.1, bf16[512,512]{1,0:T(8,128)(2,1)} %v_hbm.1, f32[3,2048]{1,0:T(4,128)} %qt_hbm.1, f32[3,512]{1,0:T(4,128)} %kt_hbm.1, f32[3,512]{1,0:T(4,128)} %vt_hbm.1), custom_call_target="tpu_custom_call" | custom-call | flops 1610612736 | bytes 5242880 | tf_op jit(solution)/shard_map/pallas_call | solution.py:400
  23.3 1.3 %copy.9 = bf16[512,2048]{1,0:T(8,128)(2,1)} copy(bf16[512,2048]{1,0:T(8,128)(2,1)S(1)} %shard_map.73) | data formatting | bytes 4194304
